TPU v7x, 32 devices: a whole 2x2x4 slice. The times are simulated.
32 devices in a mesh: tm: 16 (over z, y, x), head: 2 (over core).
Axes of the slice: x: 2, y: 2, z: 4, core: 2. Of those that a mesh axis runs over, the one named last changes fastest.
Arguments:
- merged_qkv: bfloat16 [4096, 4608], P(('tm', 'head')), may hold values from -6 to 6
- cotangent: bfloat16 [4096, 1536], P(('tm', 'head')), may hold values from -6 to 6
- stretch_start: int32 [64], P('tm'), may hold values from 0 to 63, as said below
Outputs:
- attended: bfloat16 [4096, 1536], P(('tm', 'head'))
- grad_qkv: bfloat16 [4096, 4608], P(('tm', 'head'))
Inputs may be any that keep to these rules, and one draw needn't show every extreme that they name: stretch_start[c] is the first stretch of the utterance that holds stretch c: it never falls, stretch_start[c] <= c, and it equals c or stretch_start[c - 1]; the first and the last stretch begin utterances.
All inputs are finite; a program needn't handle non-finite values.
Results may differ from a plain program's by a relative error of at most 0.014.
Values may be sent and summed in bfloat16 or wider, within the bound.
A program may use at most 128 MiB of HBM per device.

v0:
```python
import jax
import jax.numpy as jnp
from jax import lax
from jax.sharding import PartitionSpec as P

HEADS = 24
HDIM = 64
D = 1536
CH = 64
LEFT = 8


def passed_along(value, axis, steps):
    count = lax.axis_size(axis)
    initial, last = (max(0, -steps), min(count, count - steps))
    return lax.ppermute(value, axis, [(source, source + steps) for source in range(initial, last)])


def product(form, left, right):
    return jnp.einsum(form, left, right, preferred_element_type=jnp.float32)


def pick_group(stretch_count, head_count):
    limit = max(1, 12 // head_count)
    best_size = 1
    for trial in range(1, stretch_count + 1):
        if stretch_count % trial == 0 and trial <= limit:
            best_size = trial
    return best_size


def fold_windows(window_grad, group_size):
    width = LEFT + 1 + group_size
    tail = window_grad.shape[2:]
    padded = jnp.concatenate(
        [window_grad, jnp.zeros((group_size, group_size) + tail, jnp.float32)], axis=1
    )
    flat = padded.reshape((group_size * width,) + tail)[: group_size * (width - 1)]
    return jnp.sum(flat.reshape((group_size, width - 1) + tail), axis=0)


def attend_block(query_group, key_window, value_window, grad_group, allowed, score_scale):
    scores = product("gqhd,gjkhd->ghqjk", query_group, key_window) * score_scale
    allowed_mask = allowed[:, None, None, :, None]
    scores = jnp.where(allowed_mask, scores, -1e30)
    row_max = jnp.max(scores, axis=(3, 4), keepdims=True)
    expo_terms = jnp.exp(scores - row_max)
    probs = expo_terms / jnp.sum(expo_terms, axis=(3, 4), keepdims=True)
    probs_low = probs.astype(jnp.bfloat16)
    result = product("ghqjk,gjkhd->gqhd", probs_low, value_window).astype(jnp.bfloat16)
    dprob = product("gqhd,gjkhd->ghqjk", grad_group, value_window)
    delta = jnp.sum(probs * dprob, axis=(3, 4), keepdims=True)
    dscore = (probs * (dprob - delta) * score_scale).astype(jnp.bfloat16)
    grad_query = product("ghqjk,gjkhd->gqhd", dscore, key_window)
    grad_keys = product("ghqjk,gqhd->gjkhd", dscore, query_group)
    grad_values = product("ghqjk,gqhd->gjkhd", probs_low, grad_group)
    return (result, grad_query, grad_keys, grad_values)


def attend_all(
    query_rows, key_rows, value_rows, out_grads, key_prefix, value_prefix, starts, first_stretch
):
    frames, head_count, head_size = query_rows.shape
    stretch_count = frames // CH
    group_size = pick_group(stretch_count, head_count)
    score_scale = head_size ** (-0.5)
    key_blocks = jnp.concatenate([key_prefix, key_rows], axis=0).reshape(
        LEFT + stretch_count, CH, head_count, head_size
    )
    value_blocks = jnp.concatenate([value_prefix, value_rows], axis=0).reshape(
        LEFT + stretch_count, CH, head_count, head_size
    )
    query_blocks = query_rows.reshape(stretch_count, CH, head_count, head_size)
    grad_blocks = out_grads.reshape(stretch_count, CH, head_count, head_size)

    def one_group(carry, group_index):
        key_acc, value_acc = carry
        base_stretch = group_index * group_size
        key_span = lax.dynamic_slice_in_dim(key_blocks, base_stretch, group_size + LEFT, 0)
        value_span = lax.dynamic_slice_in_dim(value_blocks, base_stretch, group_size + LEFT, 0)
        key_window = jnp.stack(
            [key_span[offset : offset + group_size] for offset in range(LEFT + 1)], axis=1
        )
        value_window = jnp.stack(
            [value_span[offset : offset + group_size] for offset in range(LEFT + 1)], axis=1
        )
        query_group = lax.dynamic_slice_in_dim(query_blocks, base_stretch, group_size, 0)
        grad_group = lax.dynamic_slice_in_dim(grad_blocks, base_stretch, group_size, 0)
        start_group = lax.dynamic_slice_in_dim(starts, base_stretch, group_size, 0)
        stretch_ids = first_stretch + base_stretch + jnp.arange(group_size, dtype=jnp.int32)
        block_ids = stretch_ids[:, None] - LEFT + jnp.arange(LEFT + 1, dtype=jnp.int32)[None, :]
        allowed = block_ids >= start_group[:, None]
        result, grad_query, key_window_grad, value_window_grad = attend_block(
            query_group, key_window, value_window, grad_group, allowed, score_scale
        )
        key_add = fold_windows(key_window_grad, group_size)
        value_add = fold_windows(value_window_grad, group_size)
        key_acc = lax.dynamic_update_slice_in_dim(
            key_acc,
            lax.dynamic_slice_in_dim(key_acc, base_stretch, group_size + LEFT, 0) + key_add,
            base_stretch,
            0,
        )
        value_acc = lax.dynamic_update_slice_in_dim(
            value_acc,
            lax.dynamic_slice_in_dim(value_acc, base_stretch, group_size + LEFT, 0) + value_add,
            base_stretch,
            0,
        )
        return ((key_acc, value_acc), (result, grad_query))

    zero_acc = jnp.zeros((LEFT + stretch_count, CH, head_count, head_size), jnp.float32)
    (key_acc, value_acc), (results, grad_query) = lax.scan(
        one_group, (zero_acc, zero_acc), jnp.arange(stretch_count // group_size, dtype=jnp.int32)
    )
    span = LEFT * CH
    return (
        results.reshape(frames, head_count, head_size),
        grad_query.reshape(frames, head_count, head_size),
        key_acc.reshape(span + frames, head_count, head_size),
        value_acc.reshape(span + frames, head_count, head_size),
    )


def run_local(
    query_rows, key_rows, value_rows, out_grads, starts, first_stretch, forward_shift, return_shift
):
    frames, head_count, head_size = query_rows.shape
    span = LEFT * CH
    shift_count = -(-span // frames)
    sent_block = jnp.stack([key_rows, value_rows], axis=0).reshape(
        2, frames, head_count * head_size
    )
    received = [forward_shift(sent_block, distance) for distance in range(shift_count, 0, -1)]
    joined = jnp.concatenate(received, axis=1).reshape(2, span, head_count, head_size)
    results, grad_query, grad_keys, grad_values = attend_all(
        query_rows, key_rows, value_rows, out_grads, joined[0], joined[1], starts, first_stretch
    )
    prefix_grads = jnp.stack([grad_keys[:span], grad_values[:span]], axis=0).reshape(
        2, span, head_count * head_size
    )
    padded = jnp.concatenate(
        [
            jnp.zeros((2, shift_count * frames - span, head_count * head_size), jnp.float32),
            prefix_grads,
        ],
        axis=1,
    )
    returned = jnp.zeros((2, frames, head_count * head_size), jnp.float32)
    for distance in range(1, shift_count + 1):
        grad_piece = padded[
            :, (shift_count - distance) * frames : (shift_count - distance + 1) * frames
        ]
        returned = returned + return_shift(grad_piece, distance)
    own_grads = jnp.stack([grad_keys[span:], grad_values[span:]], axis=0).reshape(
        2, frames, head_count * head_size
    )
    own_grads = own_grads + returned
    own_grads = own_grads.reshape(2, frames, head_count, head_size)
    return (results, grad_query, own_grads[0], own_grads[1])


def shards(merged_qkv, cotangent, stretch_start):
    local_frames = merged_qkv.shape[0]
    groups = lax.axis_size("head")
    per_group = HEADS // groups
    packed = merged_qkv.reshape(local_frames, groups, per_group * 3 * HDIM)
    cot_packed = cotangent.reshape(local_frames, groups, per_group * HDIM)
    packed, cot_packed = (
        lax.all_to_all(packed, "head", split_axis=1, concat_axis=0, tiled=True),
        lax.all_to_all(cot_packed, "head", split_axis=1, concat_axis=0, tiled=True),
    )
    shard_frames = local_frames * groups
    merged = packed.reshape(shard_frames, per_group, 3, HDIM)
    out_grads = cot_packed.reshape(shard_frames, per_group, HDIM)
    first_stretch = lax.axis_index("tm") * (shard_frames // CH)

    def forward_shift(block, distance):
        return passed_along(block, "tm", distance)

    def return_shift(block, distance):
        return passed_along(block.astype(jnp.bfloat16), "tm", -distance).astype(block.dtype)

    results, grad_query, grad_keys, grad_values = run_local(
        merged[:, :, 0],
        merged[:, :, 1],
        merged[:, :, 2],
        out_grads,
        stretch_start,
        first_stretch,
        forward_shift,
        return_shift,
    )
    grad_merged = (
        jnp.stack([grad_query, grad_keys, grad_values], axis=2)
        .astype(jnp.bfloat16)
        .reshape(shard_frames, 1, per_group * 3 * HDIM)
    )
    result_packed = results.reshape(shard_frames, 1, per_group * HDIM)
    result_packed, grad_merged = (
        lax.all_to_all(result_packed, "head", split_axis=0, concat_axis=1, tiled=True),
        lax.all_to_all(grad_merged, "head", split_axis=0, concat_axis=1, tiled=True),
    )
    return (result_packed.reshape(local_frames, D), grad_merged.reshape(local_frames, 3 * D))


def solution(mesh):
    in_specs = (P(("tm", "head"), None), P(("tm", "head"), None), P("tm"))
    out_specs = (P(("tm", "head"), None), P(("tm", "head"), None))
    return jax.shard_map(shards, mesh=mesh, in_specs=in_specs, out_specs=out_specs, check_vma=False)
```

profile of v0, /device:TPU:31, one launch (start us, length us, event | category | flops | bytes accessed | tf_op | source)
XLA Modules:
  0.0 238.2 jit_solution(6260909972245010334)
XLA Ops:
  2.3 5.0 %all_to_all.60 = bf16[128,2,2304]{0,2,1:T(8,128)(2,1)S(1)} all-to-all(bf16[128,2,2304]{0,2,1:T(8,128)(2,1)S(1)} %bitcast.348), channel_id=1, replica_groups=mesh['tm'=16,'head'=2] {'head'}, dimensions={1} | all-to-all | bytes 2359296 | tf_op jit(solution)/shard_map/all_to_all | solution.py:170
  7.3 10.0 %copy.136 = bf16[2,128,1,2304]{1,0,3,2:T(2,128)(2,1)S(1)} copy(bf16[2,128,1,2304]{1,3,0,2:T(8,128)(2,1)S(1)} %bitcast.346) | data formatting | bytes 2359296 | tf_op jit(solution)/shard_map/all_to_all | solution.py:170
  22.8 3.8 %all-to-all-start.1 = ((bf16[128,2,768]{0,2,1:T(8,128)(2,1)}), bf16[128,2,768]{0,2,1:T(8,128)(2,1)S(1)}, u32[]{:S(2)}, u32[]{:S(2)}) async-start(bf16[128,2,768]{0,2,1:T(8,128)(2,1)} %bitcast.71), calls=%async_computation.1 | async-start | bytes 786432 | tf_op jit(solution)/shard_map/all_to_all | solution.py:171
  30.9 9.3 %collective-permute-done = bf16[2,256,768]{1,2,0:T(8,128)(2,1)} collective-permute-done((bf16[2,256,768]{1,2,0:T(8,128)(2,1)}, bf16[2,256,768]{1,2,0:T(8,128)(2,1)}, u32[]{:S(2)}, u32[]{:S(2)}) %collective-permute-start) | collective-permute-done | bytes 786464 | tf_op jit(solution)/shard_map/ppermute | solution.py:16
  44.1 3.2 %reshape.204 = bf16[12,64,12,64]{1,0,3,2:T(8,128)(2,1)} reshape(bf16[768,12,64]{0,2,1:T(8,128)(2,1)S(1)} %get-tuple-element.235) | data formatting | bytes 2359296 | tf_op jit(solution)/shard_map/reshape | solution.py:67
  47.3 4.1 %copy.140 = bf16[12,64,12,64]{3,1,2,0:T(8,128)(2,1)S(1)} copy(bf16[12,64,12,64]{1,0,3,2:T(8,128)(2,1)} %reshape.204) | data formatting | bytes 2359296 | tf_op jit(solution)/shard_map/while | solution.py:113
  51.4 4.7 %reshape.206 = bf16[12,64,12,64]{1,0,3,2:T(8,128)(2,1)} reshape(bf16[768,12,64]{0,2,1:T(8,128)(2,1)} %get-tuple-element.236) | data formatting | bytes 2359296 | tf_op jit(solution)/shard_map/reshape | solution.py:70
  56.1 5.1 %copy.142 = bf16[12,64,12,64]{3,1,2,0:T(8,128)(2,1)} copy(bf16[12,64,12,64]{1,0,3,2:T(8,128)(2,1)} %reshape.206) | data formatting | bytes 2359296 | tf_op jit(solution)/shard_map/while | solution.py:113
  61.2 2.8 %broadcast_in_dim.41.clone = f32[12,64,12,64]{1,3,0,2:T(8,128)} broadcast(f32[]{:T(128)} %constant.66.clone.1), dimensions={} | broadcast | bytes 2359300 | tf_op jit(solution)/shard_map/broadcast_in_dim | solution.py:112
  63.9 2.7 %broadcast_in_dim.41 = f32[12,64,12,64]{1,3,0,2:T(8,128)} broadcast(f32[]{:T(128)} %constant.66.clone.1), dimensions={} | broadcast | bytes 2359300 | tf_op jit(solution)/shard_map/broadcast_in_dim | solution.py:112
  66.7 83.8 %while.18 = (s32[]{:T(128)}, f32[12,64,12,64]{1,3,0,2:T(8,128)}, f32[12,64,12,64]{1,3,0,2:T(8,128)}, bf16[4,1,64,12,64]{2,4,3,1,0:T(8,128)(2,1)}, bf16[4,1,64,12...) while((s32[]{:T(128)}, f32[12,64,12,64]{1,3,0,2:T(8,128)}, ...), condition=%wide.region_4.5_spmd, body=%wide.region_0.4_spmd.sunk | while | flops 354383648 | bytes 112707928 | solution.py:113
  81.1 2.1 fusion.142
  85.5 2.1 copy-done
  102.1 2.1 fusion.142
  106.4 2.1 copy-done
  123.0 2.1 fusion.142
  127.4 2.1 copy-done
  138.2 2.0 fusion.143
  144.0 2.1 fusion.142
  148.3 2.1 copy-done
  150.5 2.2 slice.170
  154.9 2.2 slice.171
  160.8 19.8 %collective-permute-start.2 = (bf16[2,256,768]{1,2,0:T(8,128)(2,1)}, bf16[2,256,768]{1,2,0:T(8,128)(2,1)}, u32[]{:S(2)}, u32[]{:S(2)}) collective-permute-start(bf16[2,256,768]{1,2,0:T(8,128)(2,1)} %get-tuple-element.224), channel_id=1, source_target_pairs={{2,0},{4,2},{6,4},{8,6},{10,8},{12,10},{14,12},{16,14},{18,16},{20... | collective-permute-start | bytes 2359304 | tf_op jit(solution)/shard_map/ppermute | solution.py:16
  180.6 2.7 %collective-permute-start.3 = (bf16[2,256,768]{1,2,0:T(8,128)(2,1)}, bf16[2,256,768]{1,2,0:T(8,128)(2,1)}, u32[]{:S(2)}, u32[]{:S(2)}) collective-permute-start(bf16[2,256,768]{1,2,0:T(8,128)(2,1)} %get-tuple-element.225), channel_id=1, source_target_pairs={{4,0},{6,2},{8,4},{10,6},{12,8},{14,10},{16,12},{18,14},{20,16},{2... | collective-permute-start | bytes 2359304 | tf_op jit(solution)/shard_map/ppermute | solution.py:16
  189.8 2.6 %copy.170 = bf16[4,1,64,12,64]{4,3,2,0,1:T(8,128)(2,1)} copy(bf16[4,1,64,12,64]{2,4,3,1,0:T(8,128)(2,1)} %get-tuple-element.154) | data formatting | bytes 786432 | tf_op jit(solution)/shard_map/reshape;reshape | solution.py:199
  192.4 3.6 %reshape.217 = bf16[256,1,768]{2,1,0:T(2,128)(2,1)} reshape(bf16[4,1,64,12,64]{4,3,2,0,1:T(8,128)(2,1)} %copy.170) | data formatting | bytes 786432 | tf_op jit(solution)/shard_map/reshape;reshape | solution.py:199
  196.7 4.7 %reduce.15 = bf16[256,768]{1,0:T(8,128)(2,1)} reduce(bf16[256,1,768]{2,1,0:T(2,128)(2,1)} %reshape.217, bf16[]{:T(256)} %broadcast.72), dimensions={1}, to_apply=%reshape.217.reduce_sub_computation | reduce | bytes 786434 | tf_op jit(solution)/shard_map/reshape;reshape | solution.py:199
  203.2 7.4 %all_to_all.61 = bf16[2,2,49152]{2,1,0:T(2,128)(2,1)} all-to-all(bf16[2,2,49152]{2,1,0:T(2,128)(2,1)} %reshape.218), channel_id=1, replica_groups=mesh['tm'=16,'head'=2] {'head'}, dimensions={0} | all-to-all | bytes 786432 | tf_op jit(solution)/shard_map/all_to_all | solution.py:201
  210.7 2.0 reshape.219
  218.5 2.2 copy.147
  220.7 3.0 %stack.152 = f32[1,256,768]{1,2,0:T(8,128)} reshape(f32[4,64,12,64]{1,0,3,2:T(4,128)} %copy.147) | data formatting | bytes 1572864 | tf_op jit(solution)/shard_map/stack | solution.py:155
  230.4 4.5 %all_to_all.62 = bf16[2,2,147456]{2,1,0:T(2,128)(2,1)S(1)} all-to-all(bf16[2,2,147456]{2,1,0:T(2,128)(2,1)S(1)} %reshape.220), channel_id=1, replica_groups=mesh['tm'=16,'head'=2] {'head'}, dimensions={0} | all-to-all | bytes 2359296 | tf_op jit(solution)/shard_map/all_to_all | solution.py:202
  (258 shorter events, 93.6 us)
Async XLA Ops:
  18.1 3.8 %copy-start.8 = (bf16[128,1536]{1,0:T(8,128)(2,1)S(1)}, bf16[128,1536]{1,0:T(8,128)(2,1)}, u32[]{:S(2)}) copy-start(bf16[128,1536]{1,0:T(8,128)(2,1)} %param.6) | copy-start | bytes 1179652
  19.3 20.9 %collective-permute-start = (bf16[2,256,768]{1,2,0:T(8,128)(2,1)}, bf16[2,256,768]{1,2,0:T(8,128)(2,1)}, u32[]{:S(2)}, u32[]{:S(2)}) collective-permute-start(bf16[2,256,768]{1,2,0:T(8,128)(2,1)} %pad_maximum_fusion.3), channel_id=1, source_target_pairs={{0,4},{2,6},{4,8},{6,10},{8,12},{10,14},{12,16},{14,18},{16,20},{1... | collective-permute-start | bytes 2359304 | tf_op jit(solution)/shard_map/ppermute | solution.py:16
  20.6 21.0 %collective-permute-start.1 = (bf16[2,256,768]{1,2,0:T(8,128)(2,1)}, bf16[2,256,768]{1,2,0:T(8,128)(2,1)}, u32[]{:S(2)}, u32[]{:S(2)}) collective-permute-start(bf16[2,256,768]{1,2,0:T(8,128)(2,1)} %pad_maximum_fusion.3), channel_id=1, source_target_pairs={{0,2},{2,4},{4,6},{6,8},{8,10},{10,12},{12,14},{14,16},{16,18},{18... | collective-permute-start | bytes 2359304 | tf_op jit(solution)/shard_map/ppermute | solution.py:16
  22.8 5.1 %all-to-all-start.1 = ((bf16[128,2,768]{0,2,1:T(8,128)(2,1)}), bf16[128,2,768]{0,2,1:T(8,128)(2,1)S(1)}, u32[]{:S(2)}, u32[]{:S(2)}) async-start(bf16[128,2,768]{0,2,1:T(8,128)(2,1)} %bitcast.71), calls=%async_computation.1 | async-start | bytes 786432 | tf_op jit(solution)/shard_map/all_to_all | solution.py:171
  63.9 2.7 %copy-start.9 = (s32[4]{0:T(128)S(1)}, s32[4]{0:T(128)}, u32[]{:S(2)}) copy-start(s32[4]{0:T(128)} %param.7) | copy-start | bytes 52
  77.9 3.2 %slice-start.2 = ((s8[4718592]{0:T(1024)(128)(4,1)}), s8[4194304]{0:T(1024)(128)(4,1)S(1)}, s32[]{:S(2)}) async-start(s8[4718592]{0:T(1024)(128)(4,1)} %bitcast.342), calls=%async_computation.6 | async-start | bytes 8388608 | tf_op jit(solution)/shard_map/while
  80.3 3.0 %slice-start = ((s8[4718592]{0:T(1024)(128)(4,1)}), s8[4194304]{0:T(1024)(128)(4,1)S(1)}, s32[]{:S(2)}) async-start(s8[4718592]{0:T(1024)(128)(4,1)} %bitcast.339), calls=%async_computation.4 | async-start | bytes 8388608 | tf_op jit(solution)/shard_map/while
  81.1 2.1 copy-start.6
  81.1 2.2 slice-start.1
  83.3 2.2 copy-start.2
  85.5 2.1 copy-start
  98.8 3.2 %slice-start.2 = ((s8[4718592]{0:T(1024)(128)(4,1)}), s8[4194304]{0:T(1024)(128)(4,1)S(1)}, s32[]{:S(2)}) async-start(s8[4718592]{0:T(1024)(128)(4,1)} %bitcast.342), calls=%async_computation.6 | async-start | bytes 8388608 | tf_op jit(solution)/shard_map/while
  101.3 3.0 %slice-start = ((s8[4718592]{0:T(1024)(128)(4,1)}), s8[4194304]{0:T(1024)(128)(4,1)S(1)}, s32[]{:S(2)}) async-start(s8[4718592]{0:T(1024)(128)(4,1)} %bitcast.339), calls=%async_computation.4 | async-start | bytes 8388608 | tf_op jit(solution)/shard_map/while
  102.1 2.1 copy-start.6
  102.1 2.2 slice-start.1
  104.3 2.2 copy-start.2
  106.4 2.1 copy-start
  119.8 3.2 %slice-start.2 = ((s8[4718592]{0:T(1024)(128)(4,1)}), s8[4194304]{0:T(1024)(128)(4,1)S(1)}, s32[]{:S(2)}) async-start(s8[4718592]{0:T(1024)(128)(4,1)} %bitcast.342), calls=%async_computation.6 | async-start | bytes 8388608 | tf_op jit(solution)/shard_map/while
  122.2 3.0 %slice-start = ((s8[4718592]{0:T(1024)(128)(4,1)}), s8[4194304]{0:T(1024)(128)(4,1)S(1)}, s32[]{:S(2)}) async-start(s8[4718592]{0:T(1024)(128)(4,1)} %bitcast.339), calls=%async_computation.4 | async-start | bytes 8388608 | tf_op jit(solution)/shard_map/while
  123.0 2.1 copy-start.6
  123.0 2.2 slice-start.1
  125.2 2.2 copy-start.2
  127.4 2.1 copy-start
  140.7 3.2 %slice-start.2 = ((s8[4718592]{0:T(1024)(128)(4,1)}), s8[4194304]{0:T(1024)(128)(4,1)S(1)}, s32[]{:S(2)}) async-start(s8[4718592]{0:T(1024)(128)(4,1)} %bitcast.342), calls=%async_computation.6 | async-start | bytes 8388608 | tf_op jit(solution)/shard_map/while
  141.9 2.1 slice-start.3
  143.2 3.0 %slice-start = ((s8[4718592]{0:T(1024)(128)(4,1)}), s8[4194304]{0:T(1024)(128)(4,1)S(1)}, s32[]{:S(2)}) async-start(s8[4718592]{0:T(1024)(128)(4,1)} %bitcast.339), calls=%async_computation.4 | async-start | bytes 8388608 | tf_op jit(solution)/shard_map/while
  144.0 2.1 copy-start.6
  144.0 2.2 slice-start.1
  146.1 2.2 copy-start.2
  148.3 2.1 copy-start
  160.8 64.8 %collective-permute-start.2 = (bf16[2,256,768]{1,2,0:T(8,128)(2,1)}, bf16[2,256,768]{1,2,0:T(8,128)(2,1)}, u32[]{:S(2)}, u32[]{:S(2)}) collective-permute-start(bf16[2,256,768]{1,2,0:T(8,128)(2,1)} %get-tuple-element.224), channel_id=1, source_target_pairs={{2,0},{4,2},{6,4},{8,6},{10,8},{12,10},{14,12},{16,14},{18,16},{20... | collective-permute-start | bytes 2359304 | tf_op jit(solution)/shard_map/ppermute | solution.py:16
  180.6 45.0 %collective-permute-start.3 = (bf16[2,256,768]{1,2,0:T(8,128)(2,1)}, bf16[2,256,768]{1,2,0:T(8,128)(2,1)}, u32[]{:S(2)}, u32[]{:S(2)}) collective-permute-start(bf16[2,256,768]{1,2,0:T(8,128)(2,1)} %get-tuple-element.225), channel_id=1, source_target_pairs={{4,0},{6,2},{8,4},{10,6},{12,8},{14,10},{16,12},{18,14},{20,16},{2... | collective-permute-start | bytes 2359304 | tf_op jit(solution)/shard_map/ppermute | solution.py:16
  (17 other events, 28.8 us)
where the time goes:
time: 240 us; the launch traced here: 238 us
  local copies, waits for them, and re-layouts  103 us (43%)
  matrix products  31.9 us (13%)
  starting transfers between devices  29 us (12%)
  other arithmetic  28.6 us (12%)
  blocking collectives  17 us (7%)
  loops' own time  16.8 us (7%)
  waiting for transfers between devices  10.7 us (4%)
    dot_general x16, matrix products, product(): return jnp.einsum(form, left, right, preferred_element_type=jnp.float32)  27 us
    ppermute x4, starting transfers between devices, passed_along(): lax.ppermute(value, axis, [(source, source + steps) for source in range(i...  25.1 us
    another operation x1, loops' own time, attend_all(): lax.scan(one_group, (zero_acc, zero_acc), jnp.arange(stretch_count // gro...  16.8 us
    unnamed x20, local copies, waits for them, and re-layouts  15.4 us
    while x144, local copies, waits for them, and re-layouts  11.9 us
    while x4, local copies, waits for them, and re-layouts, attend_all(): lax.scan(one_group, (zero_acc, zero_acc), jnp.arange(stretch_count // gro...  11.1 us
    all_to_all x1, local copies, waits for them, and re-layouts, shards(): lax.all_to_all(packed, 'head', split_axis=1, concat_axis=0, tiled=True)  9.99 us
    ppermute x4, waiting for transfers between devices, passed_along(): lax.ppermute(value, axis, [(source, source + steps) for source in range(i...  9.44 us
  transfers between devices with their start and end apart: 5, of which 3 were waited for; matrix products, arithmetic and copies ran while one was open for 17% of the time, Pallas kernels for 0%

commit v1 on v0

v1 whole, which is shorter than its diff:
```python
import functools

import jax
import jax.numpy as jnp
from jax import lax
from jax.experimental import pallas as pl
from jax.experimental.pallas import tpu as pltpu
from jax.sharding import PartitionSpec as P

HEADS = 24
HDIM = 64
D = 1536
CH = 64
LEFT = 8

MESH = pl.DeviceIdType.MESH
ROWS = 128
GROUP = 4 * ROWS
SPAN = LEFT * CH
PAIR = 2 * HDIM
CHUNKS = 3
TILE = 128
WIN = SPAN + TILE
NEG = -1e30

NT = (((1,), (1,)), ((), ()))
TN = (((0,), (0,)), ((), ()))
NN = (((1,), (0,)), ((), ()))


def dot(a, b, dims):
    return lax.dot_general(a, b, dims, preferred_element_type=jnp.float32)


def kernel(n_tm, qkv_ref, cot_ref, st_ref, o_ref, gr_ref,
           qkv, cot, qs, kv, acc, dqs, ostage, gstage, rstage, ret, stsend, stbuf,
           in_s, in_r, ct_s, ct_r, halo_s, halo_r, ret_s, ret_r,
           o_s, o_r, gr_s, gr_r, loc_in, loc_ct, loc_o, loc_gr, st_s, st_r):
    tm = lax.axis_index("tm")
    head = lax.axis_index("head")
    sub = tm % 2
    other = tm + 1 - 2 * sub
    me = sub * 2 + head
    has_prev = tm >= 2
    has_next = tm < n_tm - 2
    peers = (
        ((tm, 1 - head), sub * 2 + 1 - head),
        ((other, head), (1 - sub) * 2 + head),
        ((other, 1 - head), (1 - sub) * 2 + 1 - head),
    )
    prev, nxt = (tm - 2, head), (tm + 2, head)

    def rows_of(place):
        return pl.ds(pl.multiple_of(place * ROWS, ROWS), ROWS)

    def cols_of(place, c, width):
        return pl.ds(pl.multiple_of((place * CHUNKS + c) * width, 128), width)

    def local(src, dst, sem):
        return pltpu.make_async_copy(src, dst, sem)

    def remote(src, dst, ssem, rsem, device):
        return pltpu.make_async_remote_copy(
            src_ref=src, dst_ref=dst, send_sem=ssem, recv_sem=rsem,
            device_id=device, device_id_type=MESH)

    def in_own(c):
        return local(qkv_ref.at[:, cols_of(me, c, 3 * PAIR)], qkv.at[c, rows_of(me)], loc_in.at[c])

    def ct_own(c):
        return local(cot_ref.at[:, cols_of(me, c, PAIR)], cot.at[c, rows_of(me)], loc_ct.at[c])

    def in_send(c, j):
        return remote(qkv_ref.at[:, cols_of(peers[j][1], c, 3 * PAIR)], qkv.at[c, rows_of(me)],
                      in_s.at[c, j], in_r.at[c, j], peers[j][0])

    def in_recv(c, j):
        return remote(qkv_ref.at[:, cols_of(me, c, 3 * PAIR)], qkv.at[c, rows_of(peers[j][1])],
                      in_s.at[c, j], in_r.at[c, j], peers[j][0])

    def ct_send(c, j):
        return remote(cot_ref.at[:, cols_of(peers[j][1], c, PAIR)], cot.at[c, rows_of(me)],
                      ct_s.at[c, j], ct_r.at[c, j], peers[j][0])

    def ct_recv(c, j):
        return remote(cot_ref.at[:, cols_of(me, c, PAIR)], cot.at[c, rows_of(peers[j][1])],
                      ct_s.at[c, j], ct_r.at[c, j], peers[j][0])

    def half_base(half):
        return pl.multiple_of((sub if half == 0 else 1 - sub) * (2 * ROWS), 2 * ROWS)

    def halo(c, half):
        base = half_base(half)
        return remote(kv.at[c, pl.ds(pl.multiple_of(SPAN + base, 2 * ROWS), 2 * ROWS)],
                      kv.at[c, pl.ds(base, 2 * ROWS)],
                      halo_s.at[c, half], halo_r.at[c, half], nxt)

    def back(c):
        return remote(rstage.at[c], ret.at[c], ret_s.at[c], ret_r.at[c], prev)

    def o_own(c):
        return local(ostage.at[c, rows_of(me)], o_ref.at[:, cols_of(me, c, PAIR)], loc_o.at[c])

    def o_send(c, j):
        return remote(ostage.at[c, rows_of(peers[j][1])], o_ref.at[:, cols_of(me, c, PAIR)],
                      o_s.at[c, j], o_r.at[c, j], peers[j][0])

    def o_recv(c, j):
        return remote(ostage.at[c, rows_of(me)], o_ref.at[:, cols_of(peers[j][1], c, PAIR)],
                      o_s.at[c, j], o_r.at[c, j], peers[j][0])

    def gr_own(c):
        return local(gstage.at[c, rows_of(me)], gr_ref.at[:, cols_of(me, c, 3 * PAIR)], loc_gr.at[c])

    def gr_send(c, j):
        return remote(gstage.at[c, rows_of(peers[j][1])], gr_ref.at[:, cols_of(me, c, 3 * PAIR)],
                      gr_s.at[c, j], gr_r.at[c, j], peers[j][0])

    def gr_recv(c, j):
        return remote(gstage.at[c, rows_of(me)], gr_ref.at[:, cols_of(peers[j][1], c, 3 * PAIR)],
                      gr_s.at[c, j], gr_r.at[c, j], peers[j][0])

    barrier = pltpu.get_barrier_semaphore()
    for device, _ in peers:
        pl.semaphore_signal(barrier, inc=1, device_id=device, device_id_type=MESH)

    @pl.when(has_prev)
    def _():
        pl.semaphore_signal(barrier, inc=1, device_id=prev, device_id_type=MESH)

    @pl.when(has_next)
    def _():
        pl.semaphore_signal(barrier, inc=1, device_id=nxt, device_id_type=MESH)

    for c in range(CHUNKS):
        in_own(c).start()
        ct_own(c).start()
    for s in range(4):
        stsend[s:s + 1, :] = jnp.full((1, 128), st_ref[s], jnp.int32)
    stsend[4:8, :] = jnp.zeros((4, 128), jnp.int32)

    @pl.when(jnp.logical_not(has_prev))
    def _():
        for c in range(CHUNKS):
            kv[c, 0:SPAN, :] = jnp.zeros((SPAN, 2 * PAIR), jnp.bfloat16)

    pl.semaphore_wait(barrier, 3 + has_prev.astype(jnp.int32) + has_next.astype(jnp.int32))

    own_st = pl.ds(pl.multiple_of(sub * 8, 8), 8)
    other_st = pl.ds(pl.multiple_of((1 - sub) * 8, 8), 8)
    st_copy = remote(stsend, stbuf.at[own_st], st_s, st_r, (other, head))
    st_in = remote(stsend, stbuf.at[other_st], st_s, st_r, (other, head))
    st_copy.start()
    order = ((in_send, 0), (in_send, 1), (ct_send, 0), (in_send, 2), (ct_send, 1), (ct_send, 2))
    for what, c in order:
        for j in (1, 2, 0):
            what(c, j).start()
    stbuf[own_st, :] = stsend[...]

    lane = lax.broadcasted_iota(jnp.int32, (1, PAIR), 1)
    low = lane < HDIM
    low_b = jnp.where(low, 1.0, 0.0).astype(jnp.bfloat16)
    high_b = jnp.where(low, 0.0, 1.0).astype(jnp.bfloat16)

    for c in range(CHUNKS):
        for half in range(2):
            if half == 0:
                in_own(c).wait()
                in_recv(c, 0).wait_recv()
            else:
                in_recv(c, 1).wait_recv()
                in_recv(c, 2).wait_recv()
            base = half_base(half)
            for piece in range(2):
                rows = pl.ds(pl.multiple_of(base + piece * ROWS, ROWS), ROWS)
                up = pl.ds(pl.multiple_of(SPAN + base + piece * ROWS, ROWS), ROWS)
                t0 = qkv[c, rows, 0:PAIR].astype(jnp.float32)
                t1 = qkv[c, rows, PAIR:2 * PAIR].astype(jnp.float32)
                t2 = qkv[c, rows, 2 * PAIR:3 * PAIR].astype(jnp.float32)
                qs[c, rows, :] = (jnp.where(low, t0, t1) * 0.125).astype(jnp.bfloat16)
                key = jnp.where(low, pltpu.roll(t0, HDIM, 1), pltpu.roll(t2, HDIM, 1))
                kv[c, up, 0:PAIR] = key.astype(jnp.bfloat16)
                kv[c, up, PAIR:2 * PAIR] = jnp.where(low, t1, t2).astype(jnp.bfloat16)

            @pl.when(has_next)
            def _():
                halo(c, half).start()

    st_in.wait_recv()
    base_stretch = (tm // 2) * LEFT

    def tile(c, qt):
        q_rows = pl.ds(pl.multiple_of(qt * TILE, TILE), TILE)
        k_rows = pl.ds(pl.multiple_of(qt * TILE, TILE), WIN)
        q = qs[c, q_rows, :]
        g = cot[c, q_rows, :]
        qq = jnp.concatenate([q * low_b, q * high_b], axis=0)
        gg = jnp.concatenate([g * low_b, g * high_b], axis=0)
        kw = kv[c, k_rows, 0:PAIR]
        vw = kv[c, k_rows, PAIR:2 * PAIR]
        st_row = (qt // 2) * 8 + (qt % 2) * 2
        first = jnp.where(low, stbuf[pl.ds(st_row, 1), :], stbuf[pl.ds(st_row + 1, 1), :])
        second = jnp.where(low, 0, 1)
        lo = jnp.maximum(second, first - base_stretch + LEFT - 2 * qt)
        lo = jnp.concatenate([lo, lo], axis=1)
        hi = jnp.concatenate([second, second], axis=1) + LEFT
        s = dot(kw, qq, NT)
        parts = []
        for b in range(WIN // CH):
            bias = jnp.where((lo <= b) & (hi >= b), 0.0, NEG)
            parts.append(s[b * CH:(b + 1) * CH, :] + bias)
        s = jnp.concatenate(parts, axis=0)
        e = jnp.exp(s - jnp.max(s, axis=0, keepdims=True))
        p = e * (1.0 / jnp.sum(e, axis=0, keepdims=True))
        pb = p.astype(jnp.bfloat16)
        dp = dot(vw, gg, NT)
        delta = jnp.sum(p * dp, axis=0, keepdims=True)
        ds = (p * (dp - delta)).astype(jnp.bfloat16)
        ot = dot(vw, pb, TN)
        dqt = dot(kw, ds, TN)
        ot = jnp.concatenate([ot[0:HDIM, 0:TILE], ot[HDIM:PAIR, TILE:2 * TILE]], axis=0)
        dqt = jnp.concatenate([dqt[0:HDIM, 0:TILE], dqt[HDIM:PAIR, TILE:2 * TILE]], axis=0)
        ostage[c, q_rows, :] = ot.T.astype(jnp.bfloat16)
        dqs[c, q_rows, :] = dqt.T * 0.125
        acc[c, k_rows, 0:PAIR] += dot(ds, qq, NN)
        acc[c, k_rows, PAIR:2 * PAIR] += dot(pb, gg, NN)

    for c in range(CHUNKS):
        acc[c] = jnp.zeros((SPAN + GROUP, 2 * PAIR), jnp.float32)
        ct_own(c).wait()
        for j in range(3):
            ct_recv(c, j).wait_recv()

        @pl.when(has_prev)
        def _():
            halo(c, 0).wait_recv()
            halo(c, 1).wait_recv()

        def step(qt, carry):
            tile(c, qt)
            return carry

        lax.fori_loop(0, GROUP // TILE, step, 0)

        @pl.when(has_prev)
        def _():
            rstage[c] = acc[c, 0:SPAN, :].astype(jnp.bfloat16)
            back(c).start()

        for j in (1, 2, 0):
            o_send(c, j).start()
        o_own(c).start()

    for c in range(CHUNKS):
        @pl.when(has_next)
        def _():
            back(c).wait_recv()
            acc[c, SPAN:SPAN + GROUP, :] += ret[c].astype(jnp.float32)

        for piece in range(GROUP // ROWS):
            rows = slice(piece * ROWS, (piece + 1) * ROWS)
            up = slice(SPAN + piece * ROWS, SPAN + (piece + 1) * ROWS)
            dq = dqs[c, rows, :]
            dk = pltpu.roll(acc[c, up, 0:PAIR], HDIM, 1)
            dv = acc[c, up, PAIR:2 * PAIR]
            gstage[c, rows, 0:PAIR] = jnp.where(low, dq, dk).astype(jnp.bfloat16)
            gstage[c, rows, PAIR:2 * PAIR] = jnp.where(low, dv, dq).astype(jnp.bfloat16)
            gstage[c, rows, 2 * PAIR:3 * PAIR] = jnp.where(low, dk, dv).astype(jnp.bfloat16)
        for j in (1, 2, 0):
            gr_send(c, j).start()
        gr_own(c).start()

    st_copy.wait_send()
    for c in range(CHUNKS):
        for j in range(3):
            in_send(c, j).wait_send()
            ct_send(c, j).wait_send()
            o_send(c, j).wait_send()
            o_recv(c, j).wait_recv()

        @pl.when(has_next)
        def _():
            halo(c, 0).wait_send()
            halo(c, 1).wait_send()

        @pl.when(has_prev)
        def _():
            back(c).wait_send()

        o_own(c).wait()
        gr_own(c).wait()
        for j in range(3):
            gr_send(c, j).wait_send()
            gr_recv(c, j).wait_recv()


def shards(merged_qkv, cotangent, stretch_start):
    n_tm = lax.axis_size("tm")
    dma = pltpu.SemaphoreType.DMA
    bf16, f32 = jnp.bfloat16, jnp.float32
    any_spec = pl.BlockSpec(memory_space=pl.ANY)
    return pl.pallas_call(
        functools.partial(kernel, n_tm),
        out_shape=(jax.ShapeDtypeStruct(cotangent.shape, bf16),
                   jax.ShapeDtypeStruct(merged_qkv.shape, bf16)),
        in_specs=[any_spec, any_spec, pl.BlockSpec(memory_space=pltpu.SMEM)],
        out_specs=(any_spec, any_spec),
        scratch_shapes=[
            pltpu.VMEM((CHUNKS, GROUP, 3 * PAIR), bf16),
            pltpu.VMEM((CHUNKS, GROUP, PAIR), bf16),
            pltpu.VMEM((CHUNKS, GROUP, PAIR), bf16),
            pltpu.VMEM((CHUNKS, SPAN + GROUP, 2 * PAIR), bf16),
            pltpu.VMEM((CHUNKS, SPAN + GROUP, 2 * PAIR), f32),
            pltpu.VMEM((CHUNKS, GROUP, PAIR), f32),
            pltpu.VMEM((CHUNKS, GROUP, PAIR), bf16),
            pltpu.VMEM((CHUNKS, GROUP, 3 * PAIR), bf16),
            pltpu.VMEM((CHUNKS, SPAN, 2 * PAIR), bf16),
            pltpu.VMEM((CHUNKS, SPAN, 2 * PAIR), bf16),
            pltpu.VMEM((8, 128), jnp.int32),
            pltpu.VMEM((16, 128), jnp.int32),
            dma((CHUNKS, 3)), dma((CHUNKS, 3)), dma((CHUNKS, 3)), dma((CHUNKS, 3)),
            dma((CHUNKS, 2)), dma((CHUNKS, 2)), dma((CHUNKS,)), dma((CHUNKS,)),
            dma((CHUNKS, 3)), dma((CHUNKS, 3)), dma((CHUNKS, 3)), dma((CHUNKS, 3)),
            dma((CHUNKS,)), dma((CHUNKS,)), dma((CHUNKS,)), dma((CHUNKS,)),
            dma, dma,
        ],
        compiler_params=pltpu.CompilerParams(
            collective_id=0, has_side_effects=True, vmem_limit_bytes=48 * 1024 * 1024),
        cost_estimate=pl.CostEstimate(flops=3_000_000_000, bytes_accessed=8_000_000,
                                      transcendentals=2_000_000),
    )(merged_qkv, cotangent, stretch_start)


def solution(mesh):
    in_specs = (P(("tm", "head"), None), P(("tm", "head"), None), P("tm"))
    out_specs = (P(("tm", "head"), None), P(("tm", "head"), None))
    return jax.shard_map(shards, mesh=mesh, in_specs=in_specs, out_specs=out_specs, check_vma=False)
```

time: 240 us -> 56.1 us (0.23)
  the two profiles are of different devices: /device:TPU:31 before, /device:TPU:0 now
where the time goes in v1:
time: 56.1 us; the launch traced here: 55.9 us
  Pallas kernels  50.5 us (90%)
  local copies, waits for them, and re-layouts  4.67 us (8%)
  between operations  0.65 us (1%)
    pallas_call x1, Pallas kernels, shards(): pl.pallas_call(functools.partial(kernel, n_tm), out_shape=(jax.ShapeDtype...  50.5 us
    unnamed x8, local copies, waits for them, and re-layouts  4.67 us

profile of v1, /device:TPU:0, one launch (start us, length us, event | category | flops | bytes accessed | tf_op | source)
XLA Modules:
  0.0 55.9 jit_solution(14217659255757362283)
XLA Ops:
  0.6 0.0 copy-start
  0.6 1.3 %copy-done = bf16[128,4608]{1,0:T(8,128)(2,1)S(1)} copy-done((bf16[128,4608]{1,0:T(8,128)(2,1)S(1)}, bf16[128,4608]{1,0:T(8,128)(2,1)}, u32[]{:S(2)}) %copy-start) | copy-done | bytes 1179672
  1.9 0.0 copy-start.1
  1.9 1.0 %copy-done.1 = bf16[128,1536]{1,0:T(8,128)(2,1)S(1)} copy-done((bf16[128,1536]{1,0:T(8,128)(2,1)S(1)}, bf16[128,1536]{1,0:T(8,128)(2,1)}, u32[]{:S(2)}) %copy-start.1) | copy-done | bytes 393240
  2.9 0.0 copy-start.2
  2.9 0.7 %copy-done.2 = s32[4]{0:T(128)S(1)} copy-done((s32[4]{0:T(128)S(1)}, s32[4]{0:T(128)}, u32[]{:S(2)}) %copy-start.2) | copy-done | bytes 40
  3.6 50.5 %shard_map.50 = (bf16[128,1536]{1,0:T(8,128)(2,1)S(1)}, bf16[128,4608]{1,0:T(8,128)(2,1)S(1)}) custom-call(bf16[128,4608]{1,0:T(8,128)(2,1)S(1)} %copy-done, bf16[128,1536]{1,0:T(8,128)(2,1)S(1)} %copy-done.1, s32[4]{0:T(128)S(1)} %copy-done.2), custom_call_target="tpu_custom_call" | custom-call | flops 3000000000 | bytes 8000000 | tf_op jit(solution)/shard_map/pallas_call | solution.py:302
  54.1 0.7 %copy.7 = bf16[128,1536]{1,0:T(8,128)(2,1)} copy(bf16[128,1536]{1,0:T(8,128)(2,1)S(1)} %get-tuple-element.4) | data formatting | bytes 786432
  54.9 1.0 %copy.8 = bf16[128,4608]{1,0:T(8,128)(2,1)} copy(bf16[128,4608]{1,0:T(8,128)(2,1)S(1)} %get-tuple-element.5) | data formatting | bytes 2359296
Async XLA Ops:
  0.6 1.3 %copy-start = (bf16[128,4608]{1,0:T(8,128)(2,1)S(1)}, bf16[128,4608]{1,0:T(8,128)(2,1)}, u32[]{:S(2)}) copy-start(bf16[128,4608]{1,0:T(8,128)(2,1)} %qkv_ref.1) | copy-start | bytes 3538948
  1.9 1.0 %copy-start.1 = (bf16[128,1536]{1,0:T(8,128)(2,1)S(1)}, bf16[128,1536]{1,0:T(8,128)(2,1)}, u32[]{:S(2)}) copy-start(bf16[128,1536]{1,0:T(8,128)(2,1)} %cot_ref.1) | copy-start | bytes 1179652
  2.9 0.7 %copy-start.2 = (s32[4]{0:T(128)S(1)}, s32[4]{0:T(128)}, u32[]{:S(2)}) copy-start(s32[4]{0:T(128)} %st_ref.1) | copy-start | bytes 52

commit v2 on v1

--- a/solution.py
+++ b/solution.py
@@ -240,7 +240,7 @@
             tile(c, qt)
             return carry
 
-        lax.fori_loop(0, GROUP // TILE, step, 0)
+        lax.fori_loop(0, GROUP // TILE, step, 0, unroll=4)
 
         @pl.when(has_prev)
         def _():
@@ -298,7 +298,7 @@
     n_tm = lax.axis_size("tm")
     dma = pltpu.SemaphoreType.DMA
     bf16, f32 = jnp.bfloat16, jnp.float32
-    any_spec = pl.BlockSpec(memory_space=pl.ANY)
+    any_spec = pl.BlockSpec(memory_space=pltpu.HBM)
     return pl.pallas_call(
         functools.partial(kernel, n_tm),
         out_shape=(jax.ShapeDtypeStruct(cotangent.shape, bf16),
@@ -325,7 +325,7 @@
             dma, dma,
         ],
         compiler_params=pltpu.CompilerParams(
-            collective_id=0, has_side_effects=True, vmem_limit_bytes=48 * 1024 * 1024),
+            collective_id=0, has_side_effects=True, vmem_limit_bytes=60 * 1024 * 1024),
         cost_estimate=pl.CostEstimate(flops=3_000_000_000, bytes_accessed=8_000_000,
                                       transcendentals=2_000_000),
     )(merged_qkv, cotangent, stretch_start)

time: 56.1 us -> 54.9 us (0.979)
  Pallas kernels: 50.5 us -> 49.9 us
    pallas_call x1, Pallas kernels: 50.5 us -> 49.9 us  [shards(): pl.pallas_call(functools.partial(kernel, n_tm), out_shape=(jax.ShapeDtype...]
    unnamed x8 -> x2, local copies, waits for them, and re-layouts: 4.67 us -> 4.13 us
where the time goes in v2:
time: 54.9 us; the launch traced here: 54.7 us
  Pallas kernels  49.9 us (91%)
  local copies, waits for them, and re-layouts  4.13 us (8%)
  between operations  0.64 us (1%)
    pallas_call x1, Pallas kernels, shards(): pl.pallas_call(functools.partial(kernel, n_tm), out_shape=(jax.ShapeDtype...  49.9 us
    unnamed x2, local copies, waits for them, and re-layouts  4.13 us

profile of v2, /device:TPU:0, one launch (start us, length us, event | category | flops | bytes accessed | tf_op | source)
XLA Modules:
  0.0 54.7 jit_solution(7205903553331107272)
XLA Ops:
  0.6 49.9 %shard_map.50 = (bf16[128,1536]{1,0:T(8,128)(2,1)}, bf16[128,4608]{1,0:T(8,128)(2,1)}) custom-call(bf16[128,4608]{1,0:T(8,128)(2,1)} %qkv_ref.1, bf16[128,1536]{1,0:T(8,128)(2,1)} %cot_ref.1, s32[4]{0:T(128)} %st_ref.1), custom_call_target="tpu_custom_call" | custom-call | flops 3000000000 | bytes 8000000 | tf_op jit(solution)/shard_map/pallas_call | solution.py:302
  50.5 1.8 %copy.7 = bf16[128,1536]{1,0:T(8,128)(2,1)} copy(bf16[128,1536]{1,0:T(8,128)(2,1)} %get-tuple-element.4) | data formatting | bytes 786432
  52.3 2.4 %copy.8 = bf16[128,4608]{1,0:T(8,128)(2,1)} copy(bf16[128,4608]{1,0:T(8,128)(2,1)} %get-tuple-element.5) | data formatting | bytes 2359296

commit v3 on v2

--- a/solution.py
+++ b/solution.py
@@ -33,7 +33,7 @@
 
 
 def kernel(n_tm, qkv_ref, cot_ref, st_ref, o_ref, gr_ref,
-           qkv, cot, qs, kv, acc, dqs, ostage, gstage, rstage, ret, stsend, stbuf,
+           qkv, cot, qs, kv, acc, dqs, ostage, gstage, rstage, ret, stsend, stbuf, dqr, gkr, dq_s, dq_r, loc_dq,
            in_s, in_r, ct_s, ct_r, halo_s, halo_r, ret_s, ret_r,
            o_s, o_r, gr_s, gr_r, loc_in, loc_ct, loc_o, loc_gr, st_s, st_r):
     tm = lax.axis_index("tm")
@@ -109,15 +109,26 @@
         return remote(ostage.at[c, rows_of(me)], o_ref.at[:, cols_of(peers[j][1], c, PAIR)],
                       o_s.at[c, j], o_r.at[c, j], peers[j][0])
 
+    def dq_own(c):
+        return local(dqs.at[c, rows_of(me)], dqr.at[me * CHUNKS + c], loc_dq.at[c])
+
+    def dq_send(c, j):
+        return remote(dqs.at[c, rows_of(peers[j][1])], dqr.at[me * CHUNKS + c],
+                      dq_s.at[c, j], dq_r.at[c, j], peers[j][0])
+
+    def dq_recv(c, j):
+        return remote(dqs.at[c, rows_of(me)], dqr.at[peers[j][1] * CHUNKS + c],
+                      dq_s.at[c, j], dq_r.at[c, j], peers[j][0])
+
     def gr_own(c):
-        return local(gstage.at[c, rows_of(me)], gr_ref.at[:, cols_of(me, c, 3 * PAIR)], loc_gr.at[c])
+        return local(gstage.at[c, rows_of(me)], gkr.at[me * CHUNKS + c], loc_gr.at[c])
 
     def gr_send(c, j):
-        return remote(gstage.at[c, rows_of(peers[j][1])], gr_ref.at[:, cols_of(me, c, 3 * PAIR)],
+        return remote(gstage.at[c, rows_of(peers[j][1])], gkr.at[me * CHUNKS + c],
                       gr_s.at[c, j], gr_r.at[c, j], peers[j][0])
 
     def gr_recv(c, j):
-        return remote(gstage.at[c, rows_of(me)], gr_ref.at[:, cols_of(peers[j][1], c, 3 * PAIR)],
+        return remote(gstage.at[c, rows_of(me)], gkr.at[peers[j][1] * CHUNKS + c],
                       gr_s.at[c, j], gr_r.at[c, j], peers[j][0])
 
     barrier = pltpu.get_barrier_semaphore()
@@ -221,7 +232,7 @@
         ot = jnp.concatenate([ot[0:HDIM, 0:TILE], ot[HDIM:PAIR, TILE:2 * TILE]], axis=0)
         dqt = jnp.concatenate([dqt[0:HDIM, 0:TILE], dqt[HDIM:PAIR, TILE:2 * TILE]], axis=0)
         ostage[c, q_rows, :] = ot.T.astype(jnp.bfloat16)
-        dqs[c, q_rows, :] = dqt.T * 0.125
+        dqs[c, q_rows, :] = (dqt.T * 0.125).astype(jnp.bfloat16)
         acc[c, k_rows, 0:PAIR] += dot(ds, qq, NN)
         acc[c, k_rows, PAIR:2 * PAIR] += dot(pb, gg, NN)
 
@@ -249,7 +260,9 @@
 
         for j in (1, 2, 0):
             o_send(c, j).start()
+            dq_send(c, j).start()
         o_own(c).start()
+        dq_own(c).start()
 
     for c in range(CHUNKS):
         @pl.when(has_next)
@@ -257,18 +270,20 @@
             back(c).wait_recv()
             acc[c, SPAN:SPAN + GROUP, :] += ret[c].astype(jnp.float32)
 
-        for piece in range(GROUP // ROWS):
-            rows = slice(piece * ROWS, (piece + 1) * ROWS)
-            up = slice(SPAN + piece * ROWS, SPAN + (piece + 1) * ROWS)
-            dq = dqs[c, rows, :]
-            dk = pltpu.roll(acc[c, up, 0:PAIR], HDIM, 1)
-            dv = acc[c, up, PAIR:2 * PAIR]
-            gstage[c, rows, 0:PAIR] = jnp.where(low, dq, dk).astype(jnp.bfloat16)
-            gstage[c, rows, PAIR:2 * PAIR] = jnp.where(low, dv, dq).astype(jnp.bfloat16)
-            gstage[c, rows, 2 * PAIR:3 * PAIR] = jnp.where(low, dk, dv).astype(jnp.bfloat16)
+        gstage[c] = acc[c, SPAN:SPAN + GROUP, :].astype(jnp.bfloat16)
         for j in (1, 2, 0):
             gr_send(c, j).start()
         gr_own(c).start()
+
+    def place_grads(place, c):
+        slot = place * CHUNKS + c
+        dq = dqr[slot].astype(jnp.float32)
+        dk = pltpu.roll(gkr[slot, :, 0:PAIR].astype(jnp.float32), HDIM, 1)
+        dv = gkr[slot, :, PAIR:2 * PAIR].astype(jnp.float32)
+        out = (jnp.where(low, dq, dk), jnp.where(low, dv, dq), jnp.where(low, dk, dv))
+        for part in range(3):
+            cols = pl.ds(pl.multiple_of((slot * 3 + part) * PAIR, PAIR), PAIR)
+            gr_ref[:, cols] = out[part].astype(jnp.bfloat16)
 
     st_copy.wait_send()
     for c in range(CHUNKS):
@@ -276,6 +291,7 @@
             in_send(c, j).wait_send()
             ct_send(c, j).wait_send()
             o_send(c, j).wait_send()
+            dq_send(c, j).wait_send()
             o_recv(c, j).wait_recv()
 
         @pl.when(has_next)
@@ -288,10 +304,14 @@
             back(c).wait_send()
 
         o_own(c).wait()
+        dq_own(c).wait()
         gr_own(c).wait()
-        for j in range(3):
+        place_grads(me, c)
+        for j in (0, 1, 2):
+            dq_recv(c, j).wait_recv()
+            gr_recv(c, j).wait_recv()
+            place_grads(peers[j][1], c)
             gr_send(c, j).wait_send()
-            gr_recv(c, j).wait_recv()
 
 
 def shards(merged_qkv, cotangent, stretch_start):
@@ -304,20 +324,23 @@
         out_shape=(jax.ShapeDtypeStruct(cotangent.shape, bf16),
                    jax.ShapeDtypeStruct(merged_qkv.shape, bf16)),
         in_specs=[any_spec, any_spec, pl.BlockSpec(memory_space=pltpu.SMEM)],
-        out_specs=(any_spec, any_spec),
+        out_specs=(any_spec, pl.BlockSpec(memory_space=pltpu.VMEM)),
         scratch_shapes=[
             pltpu.VMEM((CHUNKS, GROUP, 3 * PAIR), bf16),
             pltpu.VMEM((CHUNKS, GROUP, PAIR), bf16),
             pltpu.VMEM((CHUNKS, GROUP, PAIR), bf16),
             pltpu.VMEM((CHUNKS, SPAN + GROUP, 2 * PAIR), bf16),
             pltpu.VMEM((CHUNKS, SPAN + GROUP, 2 * PAIR), f32),
-            pltpu.VMEM((CHUNKS, GROUP, PAIR), f32),
             pltpu.VMEM((CHUNKS, GROUP, PAIR), bf16),
-            pltpu.VMEM((CHUNKS, GROUP, 3 * PAIR), bf16),
+            pltpu.VMEM((CHUNKS, GROUP, PAIR), bf16),
+            pltpu.VMEM((CHUNKS, GROUP, 2 * PAIR), bf16),
             pltpu.VMEM((CHUNKS, SPAN, 2 * PAIR), bf16),
             pltpu.VMEM((CHUNKS, SPAN, 2 * PAIR), bf16),
             pltpu.VMEM((8, 128), jnp.int32),
             pltpu.VMEM((16, 128), jnp.int32),
+            pltpu.VMEM((4 * CHUNKS, ROWS, PAIR), bf16),
+            pltpu.VMEM((4 * CHUNKS, ROWS, 2 * PAIR), bf16),
+            dma((CHUNKS, 3)), dma((CHUNKS, 3)), dma((CHUNKS,)),
             dma((CHUNKS, 3)), dma((CHUNKS, 3)), dma((CHUNKS, 3)), dma((CHUNKS, 3)),
             dma((CHUNKS, 2)), dma((CHUNKS, 2)), dma((CHUNKS,)), dma((CHUNKS,)),
             dma((CHUNKS, 3)), dma((CHUNKS, 3)), dma((CHUNKS, 3)), dma((CHUNKS, 3)),

time: 54.9 us -> 54.3 us (0.989)
  Pallas kernels: 49.9 us -> 49.3 us
where the time goes in v3:
time: 54.3 us; the launch traced here: 54.1 us
  Pallas kernels  49.3 us (91%)
  local copies, waits for them, and re-layouts  4.13 us (8%)
  between operations  0.64 us (1%)
    pallas_call x1, Pallas kernels, shards(): pl.pallas_call(functools.partial(kernel, n_tm), out_shape=(jax.ShapeDtype...  49.3 us
    unnamed x2, local copies, waits for them, and re-layouts  4.13 us

profile of v3, /device:TPU:0, one launch (start us, length us, event | category | flops | bytes accessed | tf_op | source)
XLA Modules:
  0.0 54.1 jit_solution(13730787868782931089)
XLA Ops:
  0.6 49.3 %shard_map.50 = (bf16[128,1536]{1,0:T(8,128)(2,1)}, bf16[128,4608]{1,0:T(8,128)(2,1)}) custom-call(bf16[128,4608]{1,0:T(8,128)(2,1)} %qkv_ref.1, bf16[128,1536]{1,0:T(8,128)(2,1)} %cot_ref.1, s32[4]{0:T(128)} %st_ref.1), custom_call_target="tpu_custom_call" | custom-call | flops 3000000000 | bytes 8000000 | tf_op jit(solution)/shard_map/pallas_call | solution.py:322
  50.0 1.8 %copy.7 = bf16[128,1536]{1,0:T(8,128)(2,1)} copy(bf16[128,1536]{1,0:T(8,128)(2,1)} %get-tuple-element.4) | data formatting | bytes 786432
  51.7 2.4 %copy.8 = bf16[128,4608]{1,0:T(8,128)(2,1)} copy(bf16[128,4608]{1,0:T(8,128)(2,1)} %get-tuple-element.5) | data formatting | bytes 2359296

commit v4 on v3

--- a/solution.py
+++ b/solution.py
@@ -253,16 +253,16 @@
 
         lax.fori_loop(0, GROUP // TILE, step, 0, unroll=4)
 
-        @pl.when(has_prev)
-        def _():
-            rstage[c] = acc[c, 0:SPAN, :].astype(jnp.bfloat16)
-            back(c).start()
-
         for j in (1, 2, 0):
             o_send(c, j).start()
             dq_send(c, j).start()
         o_own(c).start()
         dq_own(c).start()
+
+        @pl.when(has_prev)
+        def _():
+            rstage[c] = acc[c, 0:SPAN, :].astype(jnp.bfloat16)
+            back(c).start()
 
     for c in range(CHUNKS):
         @pl.when(has_next)

time: 54.3 us -> 54.4 us (level)
  no operation moved by 1% of the time
where the time goes in v4:
time: 54.4 us; the launch traced here: 54.2 us
  Pallas kernels  49.4 us (91%)
  local copies, waits for them, and re-layouts  4.13 us (8%)
  between operations  0.64 us (1%)
    pallas_call x1, Pallas kernels, shards(): pl.pallas_call(functools.partial(kernel, n_tm), out_shape=(jax.ShapeDtype...  49.4 us
    unnamed x2, local copies, waits for them, and re-layouts  4.13 us

profile of v4, /device:TPU:0, one launch (start us, length us, event | category | flops | bytes accessed | tf_op | source)
XLA Modules:
  0.0 54.2 jit_solution(9493369884758663396)
XLA Ops:
  0.6 49.4 %shard_map.50 = (bf16[128,1536]{1,0:T(8,128)(2,1)}, bf16[128,4608]{1,0:T(8,128)(2,1)}) custom-call(bf16[128,4608]{1,0:T(8,128)(2,1)} %qkv_ref.1, bf16[128,1536]{1,0:T(8,128)(2,1)} %cot_ref.1, s32[4]{0:T(128)} %st_ref.1), custom_call_target="tpu_custom_call" | custom-call | flops 3000000000 | bytes 8000000 | tf_op jit(solution)/shard_map/pallas_call | solution.py:322
  50.0 1.8 %copy.7 = bf16[128,1536]{1,0:T(8,128)(2,1)} copy(bf16[128,1536]{1,0:T(8,128)(2,1)} %get-tuple-element.4) | data formatting | bytes 786432
  51.8 2.4 %copy.8 = bf16[128,4608]{1,0:T(8,128)(2,1)} copy(bf16[128,4608]{1,0:T(8,128)(2,1)} %get-tuple-element.5) | data formatting | bytes 2359296
